TPU v7x, 32 devices: a whole 2x2x4 slice. The times are simulated.
32 devices in a mesh: groups: 2 (over x), blk: 16 (over z, y, core).
Axes of the slice: x: 2, y: 2, z: 4, core: 2. Of those that a mesh axis runs over, the one named last changes fastest.
Arguments:
- records: bfloat16 [8192, 2048], P(('groups', 'blk')), parts along dimension 0, may hold values from -6 to 6
- dest: int32 [8192, 1], P(('groups', 'blk')), parts along dimension 0, may hold values from 0 to 15; in each aligned block of 256 rows (0 to 255, 256 to 511, ...) at most 32 rows name the same one
- slot: int32 [8192, 1], P(('groups', 'blk')), parts along dimension 0, may hold values from 0 to 255
- valid: int32 [8192, 1], P(('groups', 'blk')), parts along dimension 0, may hold values from 256 to 2048
- masks: int32 [2], replicated, may hold values from 1 to 15, as said below
Outputs:
- correlations: bfloat16 [2, 4096, 128, 128], P(None, ('groups', 'blk')), parts along dimension 1
There are 2 independent parts, one for each index of `groups`. A program takes and returns all parts, laid end to end along the dimension named above; an argument that names none is the same for every part. Nothing has to cross between parts.
Inputs may be any that keep to these rules, and one draw needn't show every extreme that they name: `dest`: in the rows of one device no block is named more than 32 times. `masks`: 2 distinct numbers; one of them is 15.
All inputs are finite; a program needn't handle non-finite values.
Results may differ from a plain program's by a relative error of at most 0.0085.
Values may be sent and summed in bfloat16 or wider, within the bound.
A program may use at most 128 MiB of HBM per device.

v0:
```python
import functools
import math

import jax
import jax.numpy as jnp
import numpy as np
from jax import lax
from jax.experimental import pallas as pl
from jax.experimental.pallas import tpu as pltpu
from jax.sharding import PartitionSpec as P

CH = 128
F = 256
LAGS = 128
W = 2
EXTRA = 128
VMEM = pl.BlockSpec(memory_space=pltpu.VMEM)


def forward_table(nfft, bins):
    sample = np.arange(nfft, dtype=np.int64)[:, None]
    freq = np.arange(1, bins + 1, dtype=np.int64)[None, :]
    angle = (sample * freq % nfft).astype(np.float32) * np.float32(2.0 * math.pi / nfft)
    return np.concatenate([np.cos(angle), -np.sin(angle)], axis=1).astype(jnp.bfloat16)


def lag_table(nfft, bins, lags):
    shift = (np.arange(lags, dtype=np.int64) - lags // 2) % nfft
    freq = np.arange(1, bins + 1, dtype=np.int64)[None, :]
    angle = (freq * shift[:, None] % nfft).astype(np.float32) * np.float32(2.0 * math.pi / nfft)
    return np.concatenate([np.cos(angle), -np.sin(angle)], axis=1).astype(jnp.bfloat16)


def pack_kernel(capacity, records_ref, dest_ref, slot_ref, valid_ref, out_ref):
    held, nfft = records_ref.shape
    dest, slot, valid = dest_ref[...], slot_ref[...], valid_ref[...]
    named = lax.broadcasted_iota(jnp.int32, (held, 128), 1) == dest
    onehot = named.astype(jnp.float32)
    before = lax.broadcasted_iota(jnp.int32, (held, held), 1) < lax.broadcasted_iota(
        jnp.int32, (held, held), 0
    )
    earlier = jnp.dot(
        before.astype(jnp.float32).astype(jnp.bfloat16),
        onehot.astype(jnp.bfloat16),
        preferred_element_type=jnp.float32,
    )
    rank = jnp.sum(earlier * onehot, axis=1, keepdims=True).astype(jnp.int32)
    position = dest * capacity + rank
    spots = out_ref.shape[0]
    place = lax.broadcasted_iota(jnp.int32, (held, spots), 1) == position
    place = place.astype(jnp.float32).T.astype(jnp.bfloat16)
    window = lax.broadcasted_iota(jnp.int32, (held, nfft), 1) < valid
    masked = jnp.where(window, records_ref[...].astype(jnp.float32), 0.0).astype(jnp.bfloat16)
    out_ref[:, :nfft] = jnp.dot(place, masked, preferred_element_type=jnp.float32).astype(
        jnp.bfloat16
    )
    lane = lax.broadcasted_iota(jnp.int32, (held, EXTRA), 1)
    labels = jnp.where(lane == 0, slot, jnp.where(lane == 1, valid >> 3, valid & 7))
    labels = labels.astype(jnp.float32).astype(jnp.bfloat16)
    out_ref[:, nfft:] = jnp.dot(place, labels, preferred_element_type=jnp.float32).astype(
        jnp.bfloat16
    )


def whiten_kernel(arrived_ref, table_ref, out_ref):
    spots = arrived_ref.shape[0]
    nfft = table_ref.shape[0]
    rows = CH * W
    labels = arrived_ref[:, nfft:].astype(jnp.float32)
    valid = (labels[:, 1:2] * 8.0 + labels[:, 2:3]).astype(jnp.int32)
    slot = labels.T[0:1, :].astype(jnp.int32)
    row = (slot & (W - 1)) * CH + slot // W
    select = lax.broadcasted_iota(jnp.int32, (rows, spots), 0) == row
    select = select.astype(jnp.float32).astype(jnp.bfloat16)
    summed = jnp.dot(select, arrived_ref[:, :nfft], preferred_element_type=jnp.float32)
    window = lax.broadcasted_iota(jnp.int32, (spots, nfft), 1) < valid
    window = window.astype(jnp.float32).astype(jnp.bfloat16)
    coverage = jnp.dot(select, window, preferred_element_type=jnp.float32)
    trace = summed / jnp.maximum(coverage, 1.0)
    meansq = jnp.mean(trace * trace, axis=1, keepdims=True)
    normed = (trace * lax.rsqrt(meansq + 1e-06)).astype(jnp.bfloat16)
    spectrum = jnp.dot(normed, table_ref[...], preferred_element_type=jnp.float32)
    real_part, imag_part = spectrum[:, :F], spectrum[:, F:]
    amplitude = lax.rsqrt(jnp.maximum(real_part * real_part + imag_part * imag_part, nfft / 4.0))
    real_part = (real_part * amplitude).astype(jnp.bfloat16)
    imag_part = (imag_part * amplitude).astype(jnp.bfloat16)
    for w in range(W):
        base = 2 * F * w
        out_ref[:, base : base + F] = real_part[w * CH : (w + 1) * CH]
        out_ref[:, base + F : base + 2 * F] = imag_part[w * CH : (w + 1) * CH]


def correlate_kernel(far_round_ref, own_ref, other_ref, table_ref, out_ref, turned):
    scale = 1.0 / math.sqrt(W * F)
    cosine, sine = table_ref[:, :F], table_ref[:, F:]
    far_round = far_round_ref[0]
    slots, step = turned.shape[0], own_ref.shape[1]

    for index in range(step // 2):
        at = index % slots
        for half in range(2):
            mine = own_ref[0, index * 2 + half : index * 2 + half + 1, :].astype(jnp.bfloat16)
            rows = slice(half * LAGS, (half + 1) * LAGS)
            for w in range(W):
                base = 2 * F * w
                ur, ui = mine[:, base : base + F], mine[:, base + F : base + 2 * F]
                turned[at, rows, base : base + F] = cosine * ur + sine * ui
                turned[at, rows, base + F : base + 2 * F] = cosine * ui - sine * ur
        product = lax.dot_general(
            other_ref[...],
            turned[at],
            (((1,), (1,)), ((), ())),
            preferred_element_type=jnp.float32,
        )
        product = (product * scale).astype(jnp.bfloat16)
        for half in range(2):
            lags = slice(half * LAGS, (half + 1) * LAGS)
            out_ref[far_round, index * 2 + half] = product[:CH, lags]
            out_ref[1 - far_round, index * 2 + half] = product[CH:, lags]


def local(records, dest, slot, valid, masks):
    owners = lax.axis_size("blk")
    held, nfft = records.shape
    rounds = masks.shape[0]
    capacity = max(2, 2 * held // owners)
    spots = owners * capacity
    width = 2 * F * W
    big = pltpu.CompilerParams(vmem_limit_bytes=48 * 2**20)
    outgoing = pl.pallas_call(
        functools.partial(pack_kernel, capacity),
        out_shape=jax.ShapeDtypeStruct((spots, nfft + EXTRA), jnp.bfloat16),
        in_specs=[VMEM] * 4,
        out_specs=VMEM,
        compiler_params=big,
        name="pack",
    )(records, dest, slot, valid)
    arrived = lax.all_to_all(outgoing, "blk", split_axis=0, concat_axis=0, tiled=True)
    tile = pl.pallas_call(
        whiten_kernel,
        out_shape=jax.ShapeDtypeStruct((CH, width), jnp.bfloat16),
        in_specs=[VMEM] * 2,
        out_specs=VMEM,
        compiler_params=big,
        name="whiten",
    )(arrived, jnp.asarray(forward_table(nfft, F)))
    last = owners - 1
    top = 1 << (owners.bit_length() - 2)

    def swap(block, distance):
        return lax.ppermute(block, "blk", [(b, b ^ distance) for b in range(owners)])

    far = swap(tile, last)

    def branch(mask):
        if mask & top:
            return lambda mine, met: swap(met, last ^ mask)
        return lambda mine, met: swap(mine, mask)

    second = masks[0] ^ masks[1] ^ last
    near = lax.switch(second - 1, [branch(m) for m in range(1, last)], tile, far)
    far_round = jnp.where(masks[0] == last, 0, 1).astype(jnp.int32).reshape(1)
    other = jnp.concatenate([far, near], axis=0)
    step = 16
    return pl.pallas_call(
        correlate_kernel,
        grid=(CH // step,),
        out_shape=jax.ShapeDtypeStruct((rounds, CH, CH, LAGS), jnp.bfloat16),
        in_specs=[
            pl.BlockSpec(memory_space=pltpu.SMEM),
            pl.BlockSpec((1, step, width), lambda i: (i, 0, 0)),
            pl.BlockSpec((rounds * CH, width), lambda i: (0, 0)),
            pl.BlockSpec((LAGS, 2 * F), lambda i: (0, 0)),
        ],
        out_specs=pl.BlockSpec((rounds, step, CH, LAGS), lambda i: (0, i, 0, 0)),
        scratch_shapes=[pltpu.VMEM((4, 2 * LAGS, width), jnp.bfloat16)],
        compiler_params=big,
        name="correlate",
    )(
        far_round,
        tile.astype(jnp.float32).reshape(CH // step, step, width),
        other,
        jnp.asarray(lag_table(nfft, F, LAGS)),
    )


def solution(mesh):
    return jax.shard_map(
        local,
        mesh=mesh,
        in_specs=(
            P(("groups", "blk"), None),
            P(("groups", "blk"), None),
            P(("groups", "blk"), None),
            P(("groups", "blk"), None),
            P(),
        ),
        out_specs=P(None, ("groups", "blk"), None, None),
        check_vma=False,
    )
```

profile of v0, /device:TPU:0, one launch (start us, length us, event | category | flops | bytes accessed | tf_op | source)
XLA Modules:
  0.0 101.4 jit_solution(15582079572742865316)
XLA Ops:
  0.0 0.8 copy.8.dest_ref
  0.8 0.8 copy.9.slot_ref
  1.6 0.8 copy.10.valid_ref
  2.5 0.0 copy-start.1
  2.5 1.2 %copy-done.1 = bf16[256,2048]{1,0:T(8,128)(2,1)S(1)} copy-done((bf16[256,2048]{1,0:T(8,128)(2,1)S(1)}, bf16[256,2048]{1,0:T(8,128)(2,1)}, u32[]{:S(2)}) %copy-start.1) | copy-done | bytes 1048600
  3.7 1.3 %pack.1 = bf16[512,2176]{1,0:T(8,128)(2,1)S(1)} custom-call(bf16[256,2048]{1,0:T(8,128)(2,1)S(1)} %copy-done.1, s32[256,1]{1,0:T(8,128)S(1)} %copy.8.dest_ref, s32[256,1]{1,0:T(8,128)S(1)} %copy.9.slot_ref, s32[256,1]{1,0:T(8,128)S(1)} %copy.10.valid_ref), custom_call_target="tpu_custom_call" | custom-call | tf_op jit(solution)/shard_map/pack/pallas_call | solution.py:130
  5.0 0.0 copy-start
  5.0 59.3 %all_to_all.11 = bf16[16,32,2176]{2,1,0:T(8,128)(2,1)S(1)} all-to-all(bf16[16,32,2176]{2,1,0:T(8,128)(2,1)S(1)} %bitcast.5), channel_id=1, replica_groups=mesh['groups'=2,'blk'=16] {'blk'}, dimensions={0} | all-to-all | bytes 4456448 | tf_op jit(solution)/shard_map/all_to_all | solution.py:138
  64.2 0.0 copy-done
  64.2 0.0 copy-start.3
  64.2 0.0 copy-start.2
  64.2 2.2 %whiten.1 = bf16[128,1024]{1,0:T(8,128)(2,1)S(1)} custom-call(bf16[512,2176]{1,0:T(8,128)(2,1)S(1)} %bitcast.6, bf16[2048,512]{1,0:T(8,128)(2,1)S(1)} %copy-done), custom_call_target="tpu_custom_call" | custom-call | tf_op jit(solution)/shard_map/whiten/pallas_call | solution.py:139
  66.5 1.9 %collective-permute-start.14 = (bf16[128,1024]{1,0:T(8,128)(2,1)S(1)}, bf16[128,1024]{1,0:T(8,128)(2,1)S(1)}, u32[]{:S(2)}, u32[]{:S(2)}) collective-permute-start(bf16[128,1024]{1,0:T(8,128)(2,1)S(1)} %whiten.1), channel_id=1, source_target_pairs={{0,15},{1,14},{2,13},{3,12},{4,11},{5,10},{6,9},{7,8},{8,7},{9,6},... | collective-permute-start | bytes 786440 | tf_op jit(solution)/shard_map/ppermute | solution.py:151
  68.3 0.0 copy-done.3
  68.3 0.6 fusion
  70.7 6.8 %collective-permute-done.14 = bf16[128,1024]{1,0:T(8,128)(2,1)S(1)} collective-permute-done((bf16[128,1024]{1,0:T(8,128)(2,1)S(1)}, bf16[128,1024]{1,0:T(8,128)(2,1)S(1)}, u32[]{:S(2)}, u32[]{:S(2)}) %collective-permute-start.14) | collective-permute-done | bytes 262176 | tf_op jit(solution)/shard_map/ppermute | solution.py:151
  77.5 11.1 %conditional.1 = (bf16[128,1024]{1,0:T(8,128)(2,1)}) conditional(s32[]{:T(128)} %bitcast.3, bf16[128,1024]{1,0:T(8,128)(2,1)S(1)} %whiten.1, bf16[128,1024]{1,0:T(8,128)(2,1)S(1)} %whiten.1, bf16[128,1024]{1,0:T(8,128)(2,1)S(1)} %whiten.1, bf16[128,1024]{1,0:T(8,128)(2,1)S(1)} %whiten.1, ...), branch_computations={%region_0.0_spmd, %region_1.0_spmd, %region_2.0_spmd, %region_3.0_... | conditional | bytes 1048624 | solution.py:161
  77.5 4.5 %collective-permute-start.6 = (bf16[128,1024]{1,0:T(8,128)(2,1)S(1)}, bf16[128,1024]{1,0:T(8,128)(2,1)}, u32[]{:S(2)}, u32[]{:S(2)}) collective-permute-start(bf16[128,1024]{1,0:T(8,128)(2,1)S(1)} %param.6), channel_id=1, source_target_pairs={{0,7},{1,6},{2,5},{3,4},{4,3},{5,2},{6,1},{7,0},{8,15},{9,14},{10,... | collective-permute-start | bytes 786440 | tf_op jit(solution)/shard_map/cond/branch_6_fun/ppermute | solution.py:151
  82.1 6.5 %collective-permute-done.6 = bf16[128,1024]{1,0:T(8,128)(2,1)} collective-permute-done((bf16[128,1024]{1,0:T(8,128)(2,1)S(1)}, bf16[128,1024]{1,0:T(8,128)(2,1)}, u32[]{:S(2)}, u32[]{:S(2)}) %collective-permute-start.6) | collective-permute-done | bytes 262176 | tf_op jit(solution)/shard_map/cond/branch_6_fun/ppermute | solution.py:151
  88.6 1.0 pad_maximum_fusion.other_ref
  89.6 0.0 copy-done.2
  89.6 11.9 %correlate.1 = bf16[2,128,128,128]{3,2,1,0:T(8,128)(2,1)} custom-call(s32[1]{0:T(128)S(6)} %select_n.5.far_round_ref, f32[8,16,1024]{2,1,0:T(8,128)S(1)} %convert.1.own_ref, bf16[256,1024]{1,0:T(8,128)(2,1)S(1)} %pad_maximum_fusion.other_ref, bf16[128,512]{1,0:T(8,128)(2,1)S(1)} %copy-done.2), custom_call_target="tpu_custom_call" | custom-call | tf_op jit(solution)/shard_map/correlate/pallas_call | solution.py:165
  (1 shorter events, 0.0 us)
Async XLA Ops:
  2.5 1.2 %copy-start.1 = (bf16[256,2048]{1,0:T(8,128)(2,1)S(1)}, bf16[256,2048]{1,0:T(8,128)(2,1)}, u32[]{:S(2)}) copy-start(bf16[256,2048]{1,0:T(8,128)(2,1)} %records_ref.1) | copy-start | bytes 3145732
  5.0 59.3 %copy-start = (bf16[2048,512]{1,0:T(8,128)(2,1)S(1)}, bf16[2048,512]{1,0:T(8,128)(2,1)}, u32[]{:S(2)}) copy-start(bf16[2048,512]{1,0:T(8,128)(2,1)} %constant.21.clone.table_ref) | copy-start | bytes 6291460
  64.2 4.1 %copy-start.3 = (s32[2]{0:T(128)S(1)}, s32[2]{0:T(128)}, u32[]{:S(2)}) copy-start(s32[2]{0:T(128)} %param.25) | copy-start | bytes 28
  64.2 25.3 %copy-start.2 = (bf16[128,512]{1,0:T(8,128)(2,1)S(1)}, bf16[128,512]{1,0:T(8,128)(2,1)}, u32[]{:S(2)}) copy-start(bf16[128,512]{1,0:T(8,128)(2,1)} %constant.22.clone.table_ref) | copy-start | bytes 393220
  66.5 11.0 %collective-permute-start.14 = (bf16[128,1024]{1,0:T(8,128)(2,1)S(1)}, bf16[128,1024]{1,0:T(8,128)(2,1)S(1)}, u32[]{:S(2)}, u32[]{:S(2)}) collective-permute-start(bf16[128,1024]{1,0:T(8,128)(2,1)S(1)} %whiten.1), channel_id=1, source_target_pairs={{0,15},{1,14},{2,13},{3,12},{4,11},{5,10},{6,9},{7,8},{8,7},{9,6},... | collective-permute-start | bytes 786440 | tf_op jit(solution)/shard_map/ppermute | solution.py:151
  77.5 11.1 %collective-permute-start.6 = (bf16[128,1024]{1,0:T(8,128)(2,1)S(1)}, bf16[128,1024]{1,0:T(8,128)(2,1)}, u32[]{:S(2)}, u32[]{:S(2)}) collective-permute-start(bf16[128,1024]{1,0:T(8,128)(2,1)S(1)} %param.6), channel_id=1, source_target_pairs={{0,7},{1,6},{2,5},{3,4},{4,3},{5,2},{6,1},{7,0},{8,15},{9,14},{10,... | collective-permute-start | bytes 786440 | tf_op jit(solution)/shard_map/cond/branch_6_fun/ppermute | solution.py:151
where the time goes:
time: 102 us; the launch traced here: 101 us
  blocking collectives  59.3 us (58%)
  Pallas kernels  15.4 us (15%)
  waiting for transfers between devices  13.3 us (13%)
  starting transfers between devices  6.41 us (6%)
  local copies, waits for them, and re-layouts  4.25 us (4%)
  between operations  1.85 us (2%)
  other arithmetic  1.03 us (1%)
    all_to_all x1, blocking collectives, local(): lax.all_to_all(outgoing, 'blk', split_axis=0, concat_axis=0, tiled=True)  59.3 us
    ppermute x2, waiting for transfers between devices, swap(): lax.ppermute(block, 'blk', [(b, b ^ distance) for b in range(owners)])  13.3 us
    pallas_call x1, Pallas kernels, local(): pl.pallas_call(correlate_kernel, grid=(CH // step,), out_shape=jax.ShapeD...  11.9 us
    ppermute x2, starting transfers between devices, swap(): lax.ppermute(block, 'blk', [(b, b ^ distance) for b in range(owners)])  6.41 us
    unnamed x11, local copies, waits for them, and re-layouts  3.66 us
    pallas_call x1, Pallas kernels, local(): pl.pallas_call(whiten_kernel, out_shape=jax.ShapeDtypeStruct((CH, width),...  2.21 us
  transfers between devices with their start and end apart: 2, of which 2 were waited for; matrix products, arithmetic and copies ran while one was open for 1% of the time, Pallas kernels for 0%

commit v1 on v0

--- a/solution.py
+++ b/solution.py
@@ -31,63 +31,120 @@
     return np.concatenate([np.cos(angle), -np.sin(angle)], axis=1).astype(jnp.bfloat16)
 
 
-def pack_kernel(capacity, records_ref, dest_ref, slot_ref, valid_ref, out_ref):
+def deliver_kernel(
+    records_ref, dest_ref, slot_ref, valid_ref, table_hbm,
+    tile_ref, far_ref,
+    outgoing, arrived, summed, coverage, table, send_sem, recv_sem, own_sem, table_sem, far_sems,
+):
+    owners, capacity, wide = outgoing.shape
     held, nfft = records_ref.shape
+    me = lax.axis_index("blk")
+
+    def met(distance):
+        other = me
+        for k in range(owners.bit_length() - 1):
+            if distance >> k & 1:
+                other = other + (1 << k) * (1 - 2 * lax.rem(lax.div(me, 1 << k), 2))
+        return other
+
+    barrier = pltpu.get_barrier_semaphore()
+    for distance in range(1, owners):
+        pl.semaphore_signal(
+            barrier, inc=1, device_id={"blk": met(distance)}, device_id_type=pl.DeviceIdType.MESH
+        )
+    fetch = pltpu.make_async_copy(table_hbm, table, table_sem)
+    fetch.start()
+
     dest, slot, valid = dest_ref[...], slot_ref[...], valid_ref[...]
-    named = lax.broadcasted_iota(jnp.int32, (held, 128), 1) == dest
-    onehot = named.astype(jnp.float32)
-    before = lax.broadcasted_iota(jnp.int32, (held, held), 1) < lax.broadcasted_iota(
-        jnp.int32, (held, held), 0
+    onehot = (lax.broadcasted_iota(jnp.int32, (128, held), 0) == dest).astype(jnp.float32)
+    before = lax.broadcasted_iota(jnp.int32, (held, held), 0) < lax.broadcasted_iota(
+        jnp.int32, (held, held), 1
     )
     earlier = jnp.dot(
+        onehot.astype(jnp.bfloat16),
         before.astype(jnp.float32).astype(jnp.bfloat16),
-        onehot.astype(jnp.bfloat16),
         preferred_element_type=jnp.float32,
     )
-    rank = jnp.sum(earlier * onehot, axis=1, keepdims=True).astype(jnp.int32)
+    rank = jnp.sum(earlier * onehot, axis=0, keepdims=True).astype(jnp.int32)
     position = dest * capacity + rank
-    spots = out_ref.shape[0]
-    place = lax.broadcasted_iota(jnp.int32, (held, spots), 1) == position
-    place = place.astype(jnp.float32).T.astype(jnp.bfloat16)
-    window = lax.broadcasted_iota(jnp.int32, (held, nfft), 1) < valid
-    masked = jnp.where(window, records_ref[...].astype(jnp.float32), 0.0).astype(jnp.bfloat16)
-    out_ref[:, :nfft] = jnp.dot(place, masked, preferred_element_type=jnp.float32).astype(
-        jnp.bfloat16
-    )
-    lane = lax.broadcasted_iota(jnp.int32, (held, EXTRA), 1)
-    labels = jnp.where(lane == 0, slot, jnp.where(lane == 1, valid >> 3, valid & 7))
-    labels = labels.astype(jnp.float32).astype(jnp.bfloat16)
-    out_ref[:, nfft:] = jnp.dot(place, labels, preferred_element_type=jnp.float32).astype(
-        jnp.bfloat16
-    )
-
-
-def whiten_kernel(arrived_ref, table_ref, out_ref):
-    spots = arrived_ref.shape[0]
-    nfft = table_ref.shape[0]
+    spots = owners * capacity
+    place = lax.broadcasted_iota(jnp.int32, (spots, held), 0) == position
+    place = place.astype(jnp.float32).astype(jnp.bfloat16)
+    line = lax.broadcasted_iota(jnp.int32, (EXTRA, held), 0)
+    labels = jnp.where(line == 0, slot, jnp.where(line == 1, valid >> 3, valid & 7))
+    labels = labels.astype(jnp.float32).T.astype(jnp.bfloat16)
+    packed = jnp.dot(place, records_ref[...], preferred_element_type=jnp.float32)
+    outgoing[:, :, :nfft] = packed.astype(jnp.bfloat16).reshape(owners, capacity, nfft)
+    packed = jnp.dot(place, labels, preferred_element_type=jnp.float32)
+    outgoing[:, :, nfft:] = packed.astype(jnp.bfloat16).reshape(owners, capacity, EXTRA)
+
+    pl.semaphore_wait(barrier, owners - 1)
+    copies = {}
+    for distance in range(owners - 1, 0, -1):
+        copies[distance] = pltpu.make_async_remote_copy(
+            src_ref=outgoing.at[met(distance)],
+            dst_ref=arrived.at[me],
+            send_sem=send_sem.at[distance],
+            recv_sem=recv_sem.at[distance],
+            device_id={"blk": met(distance)},
+            device_id_type=pl.DeviceIdType.MESH,
+        )
+        copies[distance].start()
+    own = pltpu.make_async_copy(outgoing.at[me], arrived.at[me], own_sem)
+    own.start()
+
+    half = owners // 2
     rows = CH * W
-    labels = arrived_ref[:, nfft:].astype(jnp.float32)
-    valid = (labels[:, 1:2] * 8.0 + labels[:, 2:3]).astype(jnp.int32)
-    slot = labels.T[0:1, :].astype(jnp.int32)
-    row = (slot & (W - 1)) * CH + slot // W
-    select = lax.broadcasted_iota(jnp.int32, (rows, spots), 0) == row
-    select = select.astype(jnp.float32).astype(jnp.bfloat16)
-    summed = jnp.dot(select, arrived_ref[:, :nfft], preferred_element_type=jnp.float32)
-    window = lax.broadcasted_iota(jnp.int32, (spots, nfft), 1) < valid
-    window = window.astype(jnp.float32).astype(jnp.bfloat16)
-    coverage = jnp.dot(select, window, preferred_element_type=jnp.float32)
-    trace = summed / jnp.maximum(coverage, 1.0)
+
+    def stack(base):
+        block = arrived[pl.ds(base, half)].reshape(half * capacity, wide)
+        marks = block[:, nfft:].astype(jnp.float32)
+        reach = (marks[:, 1:2] * 8.0 + marks[:, 2:3]).astype(jnp.int32)
+        goal = marks.T[0:1, :].astype(jnp.int32)
+        goal = (goal & (W - 1)) * CH + lax.div(goal, W)
+        select = lax.broadcasted_iota(jnp.int32, (rows, half * capacity), 0) == goal
+        select = select.astype(jnp.float32).astype(jnp.bfloat16)
+        window = lax.broadcasted_iota(jnp.int32, (half * capacity, nfft), 1) < reach
+        window = window.astype(jnp.float32).astype(jnp.bfloat16)
+        data = block[:, :nfft] * window
+        return (
+            jnp.dot(select, data, preferred_element_type=jnp.float32),
+            jnp.dot(select, window, preferred_element_type=jnp.float32),
+        )
+
+    near_base = lax.div(me, half) * half
+    own.wait()
+    for distance in range(half - 1, 0, -1):
+        copies[distance].wait_recv()
+    summed[...], coverage[...] = stack(near_base)
+    for distance in range(owners - 1, half - 1, -1):
+        copies[distance].wait_recv()
+    total, count = stack(half - near_base)
+    trace = (summed[...] + total) / jnp.maximum(coverage[...] + count, 1.0)
     meansq = jnp.mean(trace * trace, axis=1, keepdims=True)
     normed = (trace * lax.rsqrt(meansq + 1e-06)).astype(jnp.bfloat16)
-    spectrum = jnp.dot(normed, table_ref[...], preferred_element_type=jnp.float32)
+    fetch.wait()
+    spectrum = jnp.dot(normed, table[...], preferred_element_type=jnp.float32)
     real_part, imag_part = spectrum[:, :F], spectrum[:, F:]
     amplitude = lax.rsqrt(jnp.maximum(real_part * real_part + imag_part * imag_part, nfft / 4.0))
     real_part = (real_part * amplitude).astype(jnp.bfloat16)
     imag_part = (imag_part * amplitude).astype(jnp.bfloat16)
     for w in range(W):
         base = 2 * F * w
-        out_ref[:, base : base + F] = real_part[w * CH : (w + 1) * CH]
-        out_ref[:, base + F : base + 2 * F] = imag_part[w * CH : (w + 1) * CH]
+        tile_ref[:, base : base + F] = real_part[w * CH : (w + 1) * CH]
+        tile_ref[:, base + F : base + 2 * F] = imag_part[w * CH : (w + 1) * CH]
+    across = pltpu.make_async_remote_copy(
+        src_ref=tile_ref,
+        dst_ref=far_ref,
+        send_sem=far_sems.at[0],
+        recv_sem=far_sems.at[1],
+        device_id={"blk": met(owners - 1)},
+        device_id_type=pl.DeviceIdType.MESH,
+    )
+    across.start()
+    for distance in range(owners - 1, 0, -1):
+        copies[distance].wait_send()
+    across.wait()
 
 
 def correlate_kernel(far_round_ref, own_ref, other_ref, table_ref, out_ref, turned):
@@ -123,34 +180,43 @@
     owners = lax.axis_size("blk")
     held, nfft = records.shape
     rounds = masks.shape[0]
-    capacity = max(2, 2 * held // owners)
-    spots = owners * capacity
+    capacity = max(16, 2 * held // owners)
     width = 2 * F * W
-    big = pltpu.CompilerParams(vmem_limit_bytes=48 * 2**20)
-    outgoing = pl.pallas_call(
-        functools.partial(pack_kernel, capacity),
-        out_shape=jax.ShapeDtypeStruct((spots, nfft + EXTRA), jnp.bfloat16),
-        in_specs=[VMEM] * 4,
-        out_specs=VMEM,
-        compiler_params=big,
-        name="pack",
-    )(records, dest, slot, valid)
-    arrived = lax.all_to_all(outgoing, "blk", split_axis=0, concat_axis=0, tiled=True)
-    tile = pl.pallas_call(
-        whiten_kernel,
-        out_shape=jax.ShapeDtypeStruct((CH, width), jnp.bfloat16),
-        in_specs=[VMEM] * 2,
-        out_specs=VMEM,
-        compiler_params=big,
-        name="whiten",
-    )(arrived, jnp.asarray(forward_table(nfft, F)))
+    big = pltpu.CompilerParams(vmem_limit_bytes=56 * 2**20)
+    slots = pltpu.VMEM((owners, capacity, nfft + EXTRA), jnp.bfloat16)
+    tile, far = pl.pallas_call(
+        deliver_kernel,
+        out_shape=[jax.ShapeDtypeStruct((CH, width), jnp.bfloat16)] * 2,
+        in_specs=[VMEM] * 4 + [pl.BlockSpec(memory_space=pl.ANY)],
+        out_specs=[VMEM] * 2,
+        scratch_shapes=[
+            slots,
+            slots,
+            pltpu.VMEM((CH * W, nfft), jnp.float32),
+            pltpu.VMEM((CH * W, nfft), jnp.float32),
+            pltpu.VMEM((nfft, 2 * F), jnp.bfloat16),
+            pltpu.SemaphoreType.DMA((owners,)),
+            pltpu.SemaphoreType.DMA((owners,)),
+            pltpu.SemaphoreType.DMA,
+            pltpu.SemaphoreType.DMA,
+            pltpu.SemaphoreType.DMA((2,)),
+        ],
+        compiler_params=pltpu.CompilerParams(
+            vmem_limit_bytes=56 * 2**20, collective_id=0, has_side_effects=True
+        ),
+        name="deliver",
+    )(
+        records,
+        dest.reshape(1, held),
+        slot.reshape(1, held),
+        valid.reshape(1, held),
+        jnp.asarray(forward_table(nfft, F)),
+    )
     last = owners - 1
     top = 1 << (owners.bit_length() - 2)
 
     def swap(block, distance):
         return lax.ppermute(block, "blk", [(b, b ^ distance) for b in range(owners)])
-
-    far = swap(tile, last)
 
     def branch(mask):
         if mask & top:

time: 102 us -> 97.6 us (0.957)
  Pallas kernels: 15.4 us -> 82.5 us
  blocking collectives: 59.3 us -> 0 us
  waiting for transfers between devices: 13.3 us -> 5.84 us
  starting transfers between devices: 6.41 us -> 1.94 us
  local copies, waits for them, and re-layouts: 4.25 us -> 1.31 us
  other arithmetic: 1.03 us -> 2.63 us
    pallas_call x2 -> x1, Pallas kernels: 3.49 us -> 69.6 us  [local(): pl.pallas_call(deliver_kernel, out_shape=[jax.ShapeDtypeStruct((CH, width...]
    all_to_all x1 -> x0, blocking collectives: 59.3 us -> none  [local(): lax.all_to_all(outgoing, 'blk', split_axis=0, concat_axis=0, tiled=True)]
    ppermute x2 -> x1, waiting for transfers between devices: 13.3 us -> 5.84 us  [swap(): lax.ppermute(block, 'blk', [(b, b ^ distance) for b in range(owners)])]
    ppermute x2 -> x1, starting transfers between devices: 6.41 us -> 1.94 us  [swap(): lax.ppermute(block, 'blk', [(b, b ^ distance) for b in range(owners)])]
    unnamed x11 -> x0, local copies, waits for them, and re-layouts: 3.66 us -> none
  transfers between devices with their start and end apart: 2 -> 1, of which waited for: 2 -> 1; matrix products, arithmetic and copies ran while one was open for 1% -> 0% of each run, Pallas kernels for 0% -> 0%
where the time goes in v1:
time: 97.6 us; the launch traced here: 96.2 us
  Pallas kernels  82.5 us (85%)
  waiting for transfers between devices  5.84 us (6%)
  other arithmetic  2.63 us (3%)
  starting transfers between devices  1.94 us (2%)
  between operations  1.94 us (2%)
  local copies, waits for them, and re-layouts  1.31 us (1%)
    pallas_call x1, Pallas kernels, local(): pl.pallas_call(deliver_kernel, out_shape=[jax.ShapeDtypeStruct((CH, width...  69.6 us
    pallas_call x1, Pallas kernels, local(): pl.pallas_call(correlate_kernel, grid=(CH // step,), out_shape=jax.ShapeD...  12.9 us
    ppermute x1, waiting for transfers between devices, swap(): lax.ppermute(block, 'blk', [(b, b ^ distance) for b in range(owners)])  5.84 us
  transfers between devices with their start and end apart: 1, of which 1 were waited for; matrix products, arithmetic and copies ran while one was open for 0% of the time, Pallas kernels for 0%

profile of v1, /device:TPU:0, one launch (start us, length us, event | category | flops | bytes accessed | tf_op | source)
XLA Modules:
  0.0 96.2 jit_solution(3469279863031551693)
XLA Ops:
  0.0 1.3 %fusion = (s32[1]{0:T(128)}, s32[1]{0:T(128)}) fusion(s32[2]{0:T(128)} %param.25), kind=kLoop, calls=%fused_computation.1 | loop fusion | bytes 16 | tf_op jit(solution)/shard_map/slice | solution.py:226
  3.2 69.6 %deliver.1 = (bf16[128,1024]{1,0:T(8,128)(2,1)S(1)}, bf16[128,1024]{1,0:T(8,128)(2,1)S(1)}) custom-call(bf16[256,2048]{1,0:T(8,128)(2,1)} %records_ref.1, s32[1,256]{1,0:T(1,128)} %bitcast.7, s32[1,256]{1,0:T(1,128)} %bitcast.8, s32[1,256]{1,0:T(1,128)} %bitcast.9, bf16[2048,512]{1,0:T(8,128)(2,1)} %constant.21.clone.table_hbm), custom_call_target="tpu_custom_call" | custom-call | tf_op jit(solution)/shard_map/deliver/pallas_call | solution.py:187
  72.9 7.8 %conditional.1 = (bf16[128,1024]{1,0:T(8,128)(2,1)}) conditional(s32[]{:T(128)} %bitcast.4, bf16[128,1024]{1,0:T(8,128)(2,1)S(1)} %get-tuple-element.36, bf16[128,1024]{1,0:T(8,128)(2,1)S(1)} %get-tuple-element.36, bf16[128,1024]{1,0:T(8,128)(2,1)S(1)} %get-tuple-element.36, ...), branch_computations={%region_0.0_spmd, %region_1.0_spmd, %region_2.0_spmd, %region_3.0_... | conditional | bytes 1048624 | solution.py:227
  72.9 1.9 %collective-permute-start.4 = (bf16[128,1024]{1,0:T(8,128)(2,1)S(1)}, bf16[128,1024]{1,0:T(8,128)(2,1)}, u32[]{:S(2)}, u32[]{:S(2)}) collective-permute-start(bf16[128,1024]{1,0:T(8,128)(2,1)S(1)} %param.4), channel_id=1, source_target_pairs={{0,5},{1,4},{2,7},{3,6},{4,1},{5,0},{6,3},{7,2},{8,13},{9,12},{10,... | collective-permute-start | bytes 786440 | tf_op jit(solution)/shard_map/cond/branch_4_fun/ppermute | solution.py:219
  74.8 5.8 %collective-permute-done.4 = bf16[128,1024]{1,0:T(8,128)(2,1)} collective-permute-done((bf16[128,1024]{1,0:T(8,128)(2,1)S(1)}, bf16[128,1024]{1,0:T(8,128)(2,1)}, u32[]{:S(2)}, u32[]{:S(2)}) %collective-permute-start.4) | collective-permute-done | bytes 262176 | tf_op jit(solution)/shard_map/cond/branch_4_fun/ppermute | solution.py:219
  80.7 1.8 %pad_maximum_fusion.other_ref = bf16[256,1024]{1,0:T(8,128)(2,1)} fusion(bf16[128,1024]{1,0:T(8,128)(2,1)} %get-tuple-element.40, bf16[128,1024]{1,0:T(8,128)(2,1)S(1)} %get-tuple-element.37), kind=kLoop, calls=%fused_computation | loop fusion | flops 1048576 | bytes 1048576 | tf_op jit(solution)/shard_map/concatenate | solution.py:229
  82.4 0.9 convert.1.own_ref
  83.3 12.9 %correlate.1 = bf16[2,128,128,128]{3,2,1,0:T(8,128)(2,1)} custom-call(s32[1]{0:T(128)S(6)} %select_n.5.far_round_ref, f32[8,16,1024]{2,1,0:T(8,128)} %convert.1.own_ref, bf16[256,1024]{1,0:T(8,128)(2,1)} %pad_maximum_fusion.other_ref, bf16[128,512]{1,0:T(8,128)(2,1)} %constant.22.clone.table_ref), custom_call_target="tpu_custom_call" | custom-call | tf_op jit(solution)/shard_map/correlate/pallas_call | solution.py:231
Async XLA Ops:
  72.9 7.8 %collective-permute-start.4 = (bf16[128,1024]{1,0:T(8,128)(2,1)S(1)}, bf16[128,1024]{1,0:T(8,128)(2,1)}, u32[]{:S(2)}, u32[]{:S(2)}) collective-permute-start(bf16[128,1024]{1,0:T(8,128)(2,1)S(1)} %param.4), channel_id=1, source_target_pairs={{0,5},{1,4},{2,7},{3,6},{4,1},{5,0},{6,3},{7,2},{8,13},{9,12},{10,... | collective-permute-start | bytes 786440 | tf_op jit(solution)/shard_map/cond/branch_4_fun/ppermute | solution.py:219
